TPU v7x, 256 devices: a whole 4x4x8 slice. The times are simulated.
256 devices in a mesh: dp: 16 (over z_hi, x, core), uly: 16 (over z_lo, y).
Axes of the slice: x: 4, y: 4, z: 8 (z_hi: 2, z_lo: 4; z = z_hi * 4 + z_lo), core: 2. Of those that a mesh axis runs over, the one named last changes fastest.
Arguments:
- queries: bfloat16 [16, 2048, 4096], P('dp', 'uly'), may hold values from -6 to 6
- key_rows: bfloat16 [16, 2048, 4096], P('dp', 'uly'), may hold values from -5 to 5
- value_rows: bfloat16 [16, 2048, 4096], P('dp', 'uly'), may hold values from -5 to 5
- out_grad: bfloat16 [16, 2048, 4096], P('dp', 'uly'), may hold values from -5 to 5
- prev_grads: bfloat16 [16, 5120, 4096], P('dp', None, 'uly'), may hold values from -1.5 to 1.5
Outputs:
- attended: bfloat16 [16, 2048, 4096], P('dp', 'uly')
- query_grad: bfloat16 [16, 2048, 4096], P('dp', 'uly')
- key_grad: bfloat16 [16, 2048, 4096], P('dp', 'uly')
- value_grad: bfloat16 [16, 2048, 4096], P('dp', 'uly')
- grad_sum: float32 [5120, 4096], P('dp', 'uly')
All inputs are finite; a program needn't handle non-finite values.
Results may differ from a plain program's by a relative error of at most 0.012.
Values may be sent and summed in bfloat16 or wider, within the bound.
No kernel may reach another device: no remote copies, remote signals or barrier semaphores. Data moves between devices by JAX's collectives and lax.ppermute only.
A program may use at most 128 MiB of HBM per device.

v0:
```python
import math

import jax
import jax.numpy as jnp
from jax import lax
from jax.sharding import PartitionSpec as P

HD = 128


def attend_block(query_heads, key_heads, value_heads, grad_heads):
    seq_len, head_count, head_dim = query_heads.shape
    block_rows = min(512, seq_len)
    blocks = seq_len // block_rows
    score_scale = 1.0 / math.sqrt(head_dim)
    query_tiles = query_heads.reshape(blocks, block_rows, head_count, head_dim)
    grad_tiles = grad_heads.reshape(blocks, block_rows, head_count, head_dim)

    def one_block(totals, tiles):
        key_acc, value_acc = totals
        query_tile, grad_tile = tiles
        scores = (
            jnp.einsum("qhd,khd->hqk", query_tile, key_heads, preferred_element_type=jnp.float32)
            * score_scale
        )
        row_max = jnp.max(scores, axis=-1, keepdims=True)
        shifted = jnp.exp(scores - row_max)
        prob_rows = shifted / jnp.sum(shifted, axis=-1, keepdims=True)
        prob_low = prob_rows.astype(jnp.bfloat16)
        out_tile = jnp.einsum(
            "hqk,khd->qhd", prob_low, value_heads, preferred_element_type=jnp.float32
        ).astype(jnp.bfloat16)
        dprobs = jnp.einsum(
            "qhd,khd->hqk", grad_tile, value_heads, preferred_element_type=jnp.float32
        )
        row_delta = jnp.sum(prob_rows * dprobs, axis=-1, keepdims=True)
        dscores = (prob_rows * (dprobs - row_delta) * score_scale).astype(jnp.bfloat16)
        qgrad_tile = jnp.einsum(
            "hqk,khd->qhd", dscores, key_heads, preferred_element_type=jnp.float32
        ).astype(jnp.bfloat16)
        key_acc = key_acc + jnp.einsum(
            "hqk,qhd->khd", dscores, query_tile, preferred_element_type=jnp.float32
        )
        value_acc = value_acc + jnp.einsum(
            "hqk,qhd->khd", prob_low, grad_tile, preferred_element_type=jnp.float32
        )
        return ((key_acc, value_acc), (out_tile, qgrad_tile))

    zero_acc = jnp.zeros((seq_len, head_count, head_dim), jnp.float32)
    (key_acc, value_acc), (out_tiles, qgrad_tiles) = lax.scan(
        one_block, (zero_acc, zero_acc), (query_tiles, grad_tiles)
    )
    out_heads = out_tiles.reshape(seq_len, head_count, head_dim)
    qgrad_heads = qgrad_tiles.reshape(seq_len, head_count, head_dim)
    return (out_heads, qgrad_heads, key_acc.astype(jnp.bfloat16), value_acc.astype(jnp.bfloat16))


def on_device(queries, key_rows, value_rows, out_grad, prev_grads):
    tok_rows = queries.shape[1]
    width = queries.shape[2]
    uly_count = lax.axis_size("uly")
    split_shape = (tok_rows, uly_count, width // uly_count // HD, HD)
    query_split = queries[0].reshape(split_shape)
    key_split = key_rows[0].reshape(split_shape)
    value_split = value_rows[0].reshape(split_shape)
    grad_split = out_grad[0].reshape(split_shape)
    grad_terms = prev_grads[0].astype(jnp.float32)
    grad_sum = lax.psum_scatter(
        grad_terms.astype(jnp.bfloat16), "dp", scatter_dimension=0, tiled=True
    ).astype(jnp.float32)
    query_heads, key_heads, value_heads = (
        lax.all_to_all(query_split, "uly", split_axis=1, concat_axis=0, tiled=True),
        lax.all_to_all(key_split, "uly", split_axis=1, concat_axis=0, tiled=True),
        lax.all_to_all(value_split, "uly", split_axis=1, concat_axis=0, tiled=True),
    )
    grad_heads = lax.all_to_all(grad_split, "uly", split_axis=1, concat_axis=0, tiled=True)
    out_heads, qgrad_heads, kgrad_heads, vgrad_heads = attend_block(
        query_heads[:, 0], key_heads[:, 0], value_heads[:, 0], grad_heads[:, 0]
    )
    out_tokens, qgrad_tokens, kgrad_tokens, vgrad_tokens = (
        lax.all_to_all(out_heads[:, None], "uly", split_axis=0, concat_axis=1, tiled=True),
        lax.all_to_all(qgrad_heads[:, None], "uly", split_axis=0, concat_axis=1, tiled=True),
        lax.all_to_all(kgrad_heads[:, None], "uly", split_axis=0, concat_axis=1, tiled=True),
        lax.all_to_all(vgrad_heads[:, None], "uly", split_axis=0, concat_axis=1, tiled=True),
    )
    full_shape = (1, tok_rows, width)
    return (
        out_tokens.reshape(full_shape),
        qgrad_tokens.reshape(full_shape),
        kgrad_tokens.reshape(full_shape),
        vgrad_tokens.reshape(full_shape),
        grad_sum,
    )


def solution(mesh):
    return jax.shard_map(
        on_device,
        mesh=mesh,
        in_specs=(
            P("dp", "uly", None),
            P("dp", "uly", None),
            P("dp", "uly", None),
            P("dp", "uly", None),
            P("dp", None, "uly"),
        ),
        out_specs=(
            P("dp", "uly", None),
            P("dp", "uly", None),
            P("dp", "uly", None),
            P("dp", "uly", None),
            P("dp", "uly"),
        ),
        check_vma=False,
    )
```

profile of v0, /device:TPU:64, one launch (start us, length us, event | category | flops | bytes accessed | tf_op | source)
XLA Modules:
  0.0 536.9 jit_solution(6478415748532034791)
XLA Ops:
  10.1 8.2 %all-to-all-start.3 = ((bf16[128,16,2,128]{3,0,2,1:T(8,128)(2,1)}), bf16[128,16,2,128]{3,0,2,1:T(8,128)(2,1)S(1)}, u32[]{:S(2)}, u32[]{:S(2)}) async-start(bf16[128,16,2,128]{3,0,2,1:T(8,128)(2,1)} %copy.76), calls=%async_computation.3 | async-start | bytes 2097152 | tf_op jit(solution)/shard_map/all_to_all | solution.py:74
  20.6 23.5 %all-to-all-done.3 = bf16[128,16,2,128]{3,0,2,1:T(8,128)(2,1)S(1)} async-done(((bf16[128,16,2,128]{3,0,2,1:T(8,128)(2,1)}), bf16[128,16,2,128]{3,0,2,1:T(8,128)(2,1)S(1)}, u32[]{:S(2)}, u32[]{:S(2)}) %all-to-all-start.3) | async-done | bytes 1048608 | tf_op jit(solution)/shard_map/all_to_all | solution.py:74
  51.4 22.5 %all-to-all-done.2 = bf16[128,16,2,128]{0,3,2,1:T(8,128)(2,1)S(1)} async-done(((bf16[128,16,2,128]{0,3,2,1:T(8,128)(2,1)}), bf16[128,16,2,128]{0,3,2,1:T(8,128)(2,1)S(1)}, u32[]{:S(2)}, u32[]{:S(2)}) %all-to-all-start.2) | async-done | bytes 1048608 | tf_op jit(solution)/shard_map/all_to_all | solution.py:76
  83.6 20.2 %all-to-all-done = bf16[128,16,2,128]{0,3,2,1:T(8,128)(2,1)S(1)} async-done(((bf16[128,16,2,128]{0,3,2,1:T(8,128)(2,1)}), bf16[128,16,2,128]{0,3,2,1:T(8,128)(2,1)S(1)}, u32[]{:S(2)}, u32[]{:S(2)}) %all-to-all-start) | async-done | bytes 1048608 | tf_op jit(solution)/shard_map/all_to_all | solution.py:72
  112.0 21.8 %all-to-all-done.1 = bf16[128,16,2,128]{3,0,2,1:T(8,128)(2,1)} async-done(((bf16[128,16,2,128]{3,0,2,1:T(8,128)(2,1)}), bf16[128,16,2,128]{3,0,2,1:T(8,128)(2,1)}, u32[]{:S(2)}, u32[]{:S(2)}) %all-to-all-start.1) | async-done | bytes 1048608 | tf_op jit(solution)/shard_map/all_to_all | solution.py:73
  135.1 226.3 %while.17 = (s32[]{:T(128)}, f32[2048,2,128]{0,2,1:T(8,128)}, f32[2048,2,128]{0,2,1:T(8,128)}, bf16[4,512,2,128]{3,1,0,2:T(8,128)(2,1)}, bf16[4,512,2,128]{3,1,0...) while((s32[]{:T(128)}, f32[2048,2,128]{0,2,1:T(8,128)}, ...), condition=%wide.region_4.0_spmd.clone, body=%wide.region_0.4_spmd.clone.sunk | while | flops 3267633152 | bytes 114849920 | solution.py:50
  135.1 6.8 %fusion.116 = (f32[2,512]{1,0:T(2,128)S(1)}, f32[2,512,2048]{2,1,0:T(8,128)}) fusion(bf16[2048,2,128]{2,0,1:T(8,128)(2,1)S(1)} %get-tuple-element.247, bf16[4,512,2,128]{3,1,0,2:T(8,128)(2,1)} %get-tuple-element.246, s32[]{:T(128)} %get-tuple-element.230), kind=kOutput, calls=%fused_computation.48.clone.1 | convolution fusion | flops 543164416 | bytes 9703936 | tf_op jit(solution)/shard_map/while/body/eval_jaxpr/sub | solution.py:27
  146.4 15.1 %fusion.120 = bf16[4,512,2,128]{3,1,0,2:T(8,128)(2,1)} fusion(bf16[4,512,2,128]{3,1,0,2:T(8,128)(2,1)} %get-tuple-element.234, s32[]{:T(128)} %get-tuple-element.230, bf16[2048,2,128]{2,0,1:T(8,128)(2,1)S(1)} %get-tuple-element.247, f32[2,512,2048]{2,1,0:T(8,128)} %fusion.115, f32[2,512,2048]{2,1,0:T(8,128)} %get-tuple-element.217, ...), kind=kOutput, calls=%fused_computation.22.clone.1 | convolution fusion | flops 551685120 | bytes 34873856 | tf_op jit(solution)/shard_map/while/body/eval_jaxpr/hqk,khd->qhd/dot_general | solution.py:38
  167.1 18.3 %fusion.117 = f32[2048,2,128]{0,2,1:T(8,128)} fusion(f32[2,512,2048]{2,1,0:T(8,128)} %fusion.115, f32[2048,2,128]{0,2,1:T(8,128)} %get-tuple-element.231, pred[]{:T(512)S(6)} %compare.3, bf16[4,512,2,128]{3,1,0,2:T(8,128)(2,1)} %get-tuple-element.246, s32[]{:T(128)} %get-tuple-element.230, f32[2,512,2048]{2,1,0:T(8,128)} %get-tuple-element.217, ...), kind=kOutput, calls=%fused_computation.15.clone.1 | convolution fusion | flops 552602624 | bytes 38019584 | tf_op jit(solution)/shard_map/while/body/eval_jaxpr/hqk,qhd->khd/dot_general | solution.py:41
  190.8 6.8 %fusion.116 = (f32[2,512]{1,0:T(2,128)S(1)}, f32[2,512,2048]{2,1,0:T(8,128)}) fusion(bf16[2048,2,128]{2,0,1:T(8,128)(2,1)S(1)} %get-tuple-element.247, bf16[4,512,2,128]{3,1,0,2:T(8,128)(2,1)} %get-tuple-element.246, s32[]{:T(128)} %get-tuple-element.230), kind=kOutput, calls=%fused_computation.48.clone.1 | convolution fusion | flops 543164416 | bytes 9703936 | tf_op jit(solution)/shard_map/while/body/eval_jaxpr/sub | solution.py:27
  202.0 15.1 %fusion.120 = bf16[4,512,2,128]{3,1,0,2:T(8,128)(2,1)} fusion(bf16[4,512,2,128]{3,1,0,2:T(8,128)(2,1)} %get-tuple-element.234, s32[]{:T(128)} %get-tuple-element.230, bf16[2048,2,128]{2,0,1:T(8,128)(2,1)S(1)} %get-tuple-element.247, f32[2,512,2048]{2,1,0:T(8,128)} %fusion.115, f32[2,512,2048]{2,1,0:T(8,128)} %get-tuple-element.217, ...), kind=kOutput, calls=%fused_computation.22.clone.1 | convolution fusion | flops 551685120 | bytes 34873856 | tf_op jit(solution)/shard_map/while/body/eval_jaxpr/hqk,khd->qhd/dot_general | solution.py:38
  217.1 6.2 %fusion.118 = f32[2048,2,128]{0,2,1:T(8,128)} fusion(f32[2048,2,128]{0,2,1:T(8,128)} %get-tuple-element.232, pred[]{:T(512)S(6)} %compare.3, bf16[4,512,2,128]{3,1,0,2:T(8,128)(2,1)S(1)} %get-tuple-element.248, s32[]{:T(128)} %get-tuple-element.230, f32[2,512,2048]{2,1,0:T(8,128)} %get-tuple-element.217, f32[2,512]{1,0:T(2,128)S(1)} %get-tuple-element.218), kind=kOutput, calls=%fused_computation.14.clone.1 | convolution fusion | flops 542113792 | bytes 12849157 | tf_op jit(solution)/shard_map/while/body/eval_jaxpr/hqk,qhd->khd/dot_general | solution.py:44
  223.3 19.0 %fusion.117 = f32[2048,2,128]{0,2,1:T(8,128)} fusion(f32[2,512,2048]{2,1,0:T(8,128)} %fusion.115, f32[2048,2,128]{0,2,1:T(8,128)} %get-tuple-element.231, pred[]{:T(512)S(6)} %compare.3, bf16[4,512,2,128]{3,1,0,2:T(8,128)(2,1)} %get-tuple-element.246, s32[]{:T(128)} %get-tuple-element.230, f32[2,512,2048]{2,1,0:T(8,128)} %get-tuple-element.217, ...), kind=kOutput, calls=%fused_computation.15.clone.1 | convolution fusion | flops 552602624 | bytes 38019584 | tf_op jit(solution)/shard_map/while/body/eval_jaxpr/hqk,qhd->khd/dot_general | solution.py:41
  247.7 6.8 %fusion.116 = (f32[2,512]{1,0:T(2,128)S(1)}, f32[2,512,2048]{2,1,0:T(8,128)}) fusion(bf16[2048,2,128]{2,0,1:T(8,128)(2,1)S(1)} %get-tuple-element.247, bf16[4,512,2,128]{3,1,0,2:T(8,128)(2,1)} %get-tuple-element.246, s32[]{:T(128)} %get-tuple-element.230), kind=kOutput, calls=%fused_computation.48.clone.1 | convolution fusion | flops 543164416 | bytes 9703936 | tf_op jit(solution)/shard_map/while/body/eval_jaxpr/sub | solution.py:27
  258.9 15.1 %fusion.120 = bf16[4,512,2,128]{3,1,0,2:T(8,128)(2,1)} fusion(bf16[4,512,2,128]{3,1,0,2:T(8,128)(2,1)} %get-tuple-element.234, s32[]{:T(128)} %get-tuple-element.230, bf16[2048,2,128]{2,0,1:T(8,128)(2,1)S(1)} %get-tuple-element.247, f32[2,512,2048]{2,1,0:T(8,128)} %fusion.115, f32[2,512,2048]{2,1,0:T(8,128)} %get-tuple-element.217, ...), kind=kOutput, calls=%fused_computation.22.clone.1 | convolution fusion | flops 551685120 | bytes 34873856 | tf_op jit(solution)/shard_map/while/body/eval_jaxpr/hqk,khd->qhd/dot_general | solution.py:38
  280.2 19.0 %fusion.117 = f32[2048,2,128]{0,2,1:T(8,128)} fusion(f32[2,512,2048]{2,1,0:T(8,128)} %fusion.115, f32[2048,2,128]{0,2,1:T(8,128)} %get-tuple-element.231, pred[]{:T(512)S(6)} %compare.3, bf16[4,512,2,128]{3,1,0,2:T(8,128)(2,1)} %get-tuple-element.246, s32[]{:T(128)} %get-tuple-element.230, f32[2,512,2048]{2,1,0:T(8,128)} %get-tuple-element.217, ...), kind=kOutput, calls=%fused_computation.15.clone.1 | convolution fusion | flops 552602624 | bytes 38019584 | tf_op jit(solution)/shard_map/while/body/eval_jaxpr/hqk,qhd->khd/dot_general | solution.py:41
  304.6 6.8 %fusion.116 = (f32[2,512]{1,0:T(2,128)S(1)}, f32[2,512,2048]{2,1,0:T(8,128)}) fusion(bf16[2048,2,128]{2,0,1:T(8,128)(2,1)S(1)} %get-tuple-element.247, bf16[4,512,2,128]{3,1,0,2:T(8,128)(2,1)} %get-tuple-element.246, s32[]{:T(128)} %get-tuple-element.230), kind=kOutput, calls=%fused_computation.48.clone.1 | convolution fusion | flops 543164416 | bytes 9703936 | tf_op jit(solution)/shard_map/while/body/eval_jaxpr/sub | solution.py:27
  315.9 15.1 %fusion.120 = bf16[4,512,2,128]{3,1,0,2:T(8,128)(2,1)} fusion(bf16[4,512,2,128]{3,1,0,2:T(8,128)(2,1)} %get-tuple-element.234, s32[]{:T(128)} %get-tuple-element.230, bf16[2048,2,128]{2,0,1:T(8,128)(2,1)S(1)} %get-tuple-element.247, f32[2,512,2048]{2,1,0:T(8,128)} %fusion.115, f32[2,512,2048]{2,1,0:T(8,128)} %get-tuple-element.217, ...), kind=kOutput, calls=%fused_computation.22.clone.1 | convolution fusion | flops 551685120 | bytes 34873856 | tf_op jit(solution)/shard_map/while/body/eval_jaxpr/hqk,khd->qhd/dot_general | solution.py:38
  337.1 19.0 %fusion.117 = f32[2048,2,128]{0,2,1:T(8,128)} fusion(f32[2,512,2048]{2,1,0:T(8,128)} %fusion.115, f32[2048,2,128]{0,2,1:T(8,128)} %get-tuple-element.231, pred[]{:T(512)S(6)} %compare.3, bf16[4,512,2,128]{3,1,0,2:T(8,128)(2,1)} %get-tuple-element.246, s32[]{:T(128)} %get-tuple-element.230, f32[2,512,2048]{2,1,0:T(8,128)} %get-tuple-element.217, ...), kind=kOutput, calls=%fused_computation.15.clone.1 | convolution fusion | flops 552602624 | bytes 38019584 | tf_op jit(solution)/shard_map/while/body/eval_jaxpr/hqk,qhd->khd/dot_general | solution.py:41
  373.8 21.1 %all-to-all-done.4 = bf16[2048,1,2,128]{3,2,1,0:T(2,128)(2,1)S(1)} async-done(((bf16[2048,1,2,128]{3,2,1,0:T(2,128)(2,1)}), bf16[2048,1,2,128]{3,2,1,0:T(2,128)(2,1)S(1)}, u32[]{:S(2)}, u32[]{:S(2)}) %all-to-all-start.4) | async-done | bytes 1048608 | tf_op jit(solution)/shard_map/all_to_all | solution.py:81
  403.8 21.0 %all-to-all-done.5 = bf16[2048,1,2,128]{3,2,1,0:T(2,128)(2,1)S(1)} async-done(((bf16[2048,1,2,128]{3,2,1,0:T(2,128)(2,1)}), bf16[2048,1,2,128]{3,2,1,0:T(2,128)(2,1)S(1)}, u32[]{:S(2)}, u32[]{:S(2)}) %all-to-all-start.5) | async-done | bytes 1048608 | tf_op jit(solution)/shard_map/all_to_all | solution.py:82
  434.4 20.4 %all-to-all-done.6 = bf16[2048,1,2,128]{3,2,1,0:T(2,128)(2,1)} async-done(((bf16[2048,1,2,128]{3,2,1,0:T(2,128)(2,1)}), bf16[2048,1,2,128]{3,2,1,0:T(2,128)(2,1)}, u32[]{:S(2)}, u32[]{:S(2)}) %all-to-all-start.6) | async-done | bytes 1048608 | tf_op jit(solution)/shard_map/all_to_all | solution.py:83
  469.7 29.1 %all-to-all-done.7 = bf16[2048,1,2,128]{3,2,1,0:T(2,128)(2,1)S(1)} async-done(((bf16[2048,1,2,128]{3,2,1,0:T(2,128)(2,1)}), bf16[2048,1,2,128]{3,2,1,0:T(2,128)(2,1)S(1)}, u32[]{:S(2)}, u32[]{:S(2)}) %all-to-all-start.7) | async-done | bytes 1048608 | tf_op jit(solution)/shard_map/all_to_all | solution.py:84
  501.1 27.3 %reduce-scatter.2.cloned.1.call-done = bf16[320,256]{1,0:T(8,128)(2,1)} async-done(((bf16[5120,256]{1,0:T(8,128)(2,1)}), bf16[320,256]{1,0:T(8,128)(2,1)}) %reduce-scatter.2.cloned.1.call-update) | async-done | bytes 163856 | tf_op jit(solution)/shard_map/reduce_scatter | solution.py:68
  (53 shorter events, 138.7 us)
Async XLA Ops:
  10.1 34.0 %all-to-all-start.3 = ((bf16[128,16,2,128]{3,0,2,1:T(8,128)(2,1)}), bf16[128,16,2,128]{3,0,2,1:T(8,128)(2,1)S(1)}, u32[]{:S(2)}, u32[]{:S(2)}) async-start(bf16[128,16,2,128]{3,0,2,1:T(8,128)(2,1)} %copy.76), calls=%async_computation.3 | async-start | bytes 2097152 | tf_op jit(solution)/shard_map/all_to_all | solution.py:74
  44.1 29.9 %all-to-all-start.2 = ((bf16[128,16,2,128]{0,3,2,1:T(8,128)(2,1)}), bf16[128,16,2,128]{0,3,2,1:T(8,128)(2,1)S(1)}, u32[]{:S(2)}, u32[]{:S(2)}) async-start(bf16[128,16,2,128]{0,3,2,1:T(8,128)(2,1)} %bitcast.8), calls=%async_computation.2 | async-start | bytes 2097152 | tf_op jit(solution)/shard_map/all_to_all | solution.py:76
  73.9 29.9 %all-to-all-start = ((bf16[128,16,2,128]{0,3,2,1:T(8,128)(2,1)}), bf16[128,16,2,128]{0,3,2,1:T(8,128)(2,1)S(1)}, u32[]{:S(2)}, u32[]{:S(2)}) async-start(bf16[128,16,2,128]{0,3,2,1:T(8,128)(2,1)} %bitcast.129), calls=%async_computation | async-start | bytes 2097152 | tf_op jit(solution)/shard_map/all_to_all | solution.py:72
  103.8 5.2 copy-start
  103.8 30.0 %all-to-all-start.1 = ((bf16[128,16,2,128]{3,0,2,1:T(8,128)(2,1)}), bf16[128,16,2,128]{3,0,2,1:T(8,128)(2,1)}, u32[]{:S(2)}, u32[]{:S(2)}) async-start(bf16[128,16,2,128]{3,0,2,1:T(8,128)(2,1)} %copy.71), calls=%async_computation.1 | async-start | bytes 2097152 | tf_op jit(solution)/shard_map/all_to_all | solution.py:73
  365.1 29.9 %all-to-all-start.4 = ((bf16[2048,1,2,128]{3,2,1,0:T(2,128)(2,1)}), bf16[2048,1,2,128]{3,2,1,0:T(2,128)(2,1)S(1)}, u32[]{:S(2)}, u32[]{:S(2)}) async-start(bf16[2048,1,2,128]{3,2,1,0:T(2,128)(2,1)} %copy.81), calls=%async_computation.4 | async-start | bytes 2097152 | tf_op jit(solution)/shard_map/all_to_all | solution.py:81
  395.0 29.9 %all-to-all-start.5 = ((bf16[2048,1,2,128]{3,2,1,0:T(2,128)(2,1)}), bf16[2048,1,2,128]{3,2,1,0:T(2,128)(2,1)S(1)}, u32[]{:S(2)}, u32[]{:S(2)}) async-start(bf16[2048,1,2,128]{3,2,1,0:T(2,128)(2,1)} %copy.85), calls=%async_computation.5 | async-start | bytes 2097152 | tf_op jit(solution)/shard_map/all_to_all | solution.py:82
  424.8 30.0 %all-to-all-start.6 = ((bf16[2048,1,2,128]{3,2,1,0:T(2,128)(2,1)}), bf16[2048,1,2,128]{3,2,1,0:T(2,128)(2,1)}, u32[]{:S(2)}, u32[]{:S(2)}) async-start(bf16[2048,1,2,128]{3,2,1,0:T(2,128)(2,1)} %bitcast.126), calls=%async_computation.6 | async-start | bytes 2097152 | tf_op jit(solution)/shard_map/all_to_all | solution.py:83
  430.0 98.5 %reduce-scatter.2.cloned.1.call-start = ((), (), s32[]{:S(2)}) async-start(), calls=%async_computation.9 | async-start | bytes 2785280 | tf_op jit(solution)/shard_map/reduce_scatter | solution.py:68
  454.8 43.9 %all-to-all-start.7 = ((bf16[2048,1,2,128]{3,2,1,0:T(2,128)(2,1)}), bf16[2048,1,2,128]{3,2,1,0:T(2,128)(2,1)S(1)}, u32[]{:S(2)}, u32[]{:S(2)}) async-start(bf16[2048,1,2,128]{3,2,1,0:T(2,128)(2,1)} %bitcast.125), calls=%async_computation.7 | async-start | bytes 2097152 | tf_op jit(solution)/shard_map/all_to_all | solution.py:84
Sparse Core Ops, SparseCore 0:
  435.1 93.3 reduce-scatter.1
where the time goes:
time: 541 us; the launch traced here: 537 us
  matrix products  226 us (42%)
  waiting for transfers between devices  208 us (38%)
  starting transfers between devices  44.1 us (8%)
  local copies, waits for them, and re-layouts  39.6 us (7%)
  between operations  14.1 us (3%)
    dot_general x4, matrix products, one_block(): jnp.einsum('hqk,qhd->khd', dscores, query_tile, preferred_element_type=jn...  75.3 us
    dot_general x4, matrix products, one_block(): jnp.einsum('hqk,khd->qhd', dscores, key_heads, preferred_element_type=jnp...  60.3 us
    all_to_all x1, waiting for transfers between devices, on_device(): lax.all_to_all(vgrad_heads[:, None], 'uly', split_axis=0, concat_axis=1,...  29.1 us
    reduce_scatter x1, waiting for transfers between devices, on_device(): lax.psum_scatter(grad_terms.astype(jnp.bfloat16), 'dp', scatter_dimension...  27.3 us
    sub x4, matrix products, one_block(): shifted = jnp.exp(scores - row_max)  27.1 us
    dot_general x4, matrix products, one_block(): jnp.einsum('hqk,qhd->khd', prob_low, grad_tile, preferred_element_type=jn...  24.2 us
    all_to_all x1, waiting for transfers between devices, on_device(): lax.all_to_all(value_split, 'uly', split_axis=1, concat_axis=0, tiled=True)  23.5 us
    all_to_all x1, waiting for transfers between devices, on_device(): lax.all_to_all(grad_split, 'uly', split_axis=1, concat_axis=0, tiled=True)  22.5 us
  transfers between devices with their start and end apart: 9, of which 9 were waited for; matrix products, arithmetic and copies ran while one was open for 7% of the time, Pallas kernels for 0%

commit v1 on v0

v1 whole, which is shorter than its diff:
```python
import functools
import math

import jax
import jax.numpy as jnp
from jax import lax
from jax.experimental import pallas as pl
from jax.experimental.pallas import tpu as pltpu
from jax.sharding import PartitionSpec as P

HD = 128
SCORE_SCALE = 1.0 / math.sqrt(HD)
LOG2_E = math.log2(math.e)


def dot(left, right, left_dim, right_dim):
    return lax.dot_general(
        left,
        right,
        (((left_dim,), (right_dim,)), ((), ())),
        preferred_element_type=jnp.float32,
    )


def attend_body(block_chunks, in_ref, out_ref, kgrad_acc, vgrad_acc):
    step = pl.program_id(0)
    chunks, _, tok_rows, _ = in_ref.shape
    seq_len = chunks * tok_rows
    block_rows = block_chunks * tok_rows

    @pl.when(step == 0)
    def _():
        kgrad_acc[...] = jnp.zeros_like(kgrad_acc)
        vgrad_acc[...] = jnp.zeros_like(vgrad_acc)

    rows = pl.ds(step * block_chunks, block_chunks)
    query = in_ref[rows, 0].reshape(block_rows, HD)
    grad = in_ref[rows, 3].reshape(block_rows, HD)
    key = in_ref[:, 1].reshape(seq_len, HD)
    value = in_ref[:, 2].reshape(seq_len, HD)

    scores = dot(query, key, 1, 1)
    row_max = jnp.max(scores, axis=1, keepdims=True)
    shifted = jnp.exp2((scores - row_max) * (SCORE_SCALE * LOG2_E))
    inverse = 1.0 / jnp.sum(shifted, axis=1, keepdims=True)
    shifted_low = shifted.astype(jnp.bfloat16)
    attended = dot(shifted_low, value, 1, 0) * inverse
    grad_wide = grad.astype(jnp.float32)
    row_delta = jnp.sum(grad_wide * attended, axis=1, keepdims=True)
    dprobs = dot(grad, value, 1, 1)
    dscores = (shifted * (dprobs - row_delta)).astype(jnp.bfloat16)
    inverse_scaled = inverse * SCORE_SCALE
    query_grad = dot(dscores, key, 1, 0) * inverse_scaled
    vgrad_acc[...] += dot((grad_wide * inverse).astype(jnp.bfloat16), shifted_low, 0, 0)
    kgrad_acc[...] += dot(
        (query.astype(jnp.float32) * inverse_scaled).astype(jnp.bfloat16), dscores, 0, 0
    )
    out_ref[rows, 0] = attended.astype(jnp.bfloat16).reshape(block_chunks, tok_rows, HD)
    out_ref[rows, 1] = query_grad.astype(jnp.bfloat16).reshape(block_chunks, tok_rows, HD)

    @pl.when(step == pl.num_programs(0) - 1)
    def _():
        out_ref[:, 2] = kgrad_acc[...].T.astype(jnp.bfloat16).reshape(chunks, tok_rows, HD)
        out_ref[:, 3] = vgrad_acc[...].T.astype(jnp.bfloat16).reshape(chunks, tok_rows, HD)


def attend_head(packed):
    chunks, _, tok_rows, _ = packed.shape
    seq_len = chunks * tok_rows
    block_chunks = max(1, min(chunks, 512 // tok_rows))
    return pl.pallas_call(
        functools.partial(attend_body, block_chunks),
        grid=(chunks // block_chunks,),
        in_specs=[pl.BlockSpec(packed.shape, lambda step: (0, 0, 0, 0))],
        out_specs=pl.BlockSpec(packed.shape, lambda step: (0, 0, 0, 0)),
        out_shape=jax.ShapeDtypeStruct(packed.shape, jnp.bfloat16),
        scratch_shapes=[
            pltpu.VMEM((HD, seq_len), jnp.float32),
            pltpu.VMEM((HD, seq_len), jnp.float32),
        ],
        compiler_params=pltpu.CompilerParams(vmem_limit_bytes=60 * 1024 * 1024),
        cost_estimate=pl.CostEstimate(
            flops=12 * seq_len * seq_len * HD,
            bytes_accessed=4 * packed.size,
            transcendentals=seq_len * seq_len,
        ),
        name="attend_head",
    )(packed)


def pack_body(*refs):
    *in_refs, out_ref = refs
    for j, in_ref in enumerate(in_refs):
        for target in range(out_ref.shape[0]):
            out_ref[target, j] = in_ref[0, :, target * HD : (target + 1) * HD]


def pack_heads(arrays, first, count, step_heads):
    tok_rows = arrays[0].shape[1]
    offset = first // step_heads
    return pl.pallas_call(
        pack_body,
        grid=(count // step_heads,),
        in_specs=[
            pl.BlockSpec((1, tok_rows, step_heads * HD), lambda step: (0, 0, offset + step))
        ]
        * len(arrays),
        out_specs=pl.BlockSpec(
            (step_heads, len(arrays), tok_rows, HD), lambda step: (step, 0, 0, 0)
        ),
        out_shape=jax.ShapeDtypeStruct((count, len(arrays), tok_rows, HD), jnp.bfloat16),
        compiler_params=pltpu.CompilerParams(vmem_limit_bytes=60 * 1024 * 1024),
        name="pack_heads",
    )(*arrays)


def unpack_body(count, in_ref, *refs):
    for j, out_ref in enumerate(refs[-count:]):
        for source in range(in_ref.shape[0]):
            out_ref[0, :, source * HD : (source + 1) * HD] = in_ref[source, j]


def unpack_heads(returned, previous, first, width, step_heads):
    heads, count, tok_rows, _ = returned.shape
    offset = first // step_heads
    return pl.pallas_call(
        functools.partial(unpack_body, count),
        grid=(heads // step_heads,),
        in_specs=[
            pl.BlockSpec((step_heads, count, tok_rows, HD), lambda step: (step, 0, 0, 0))
        ]
        + [pl.BlockSpec(memory_space=pl.ANY)] * len(previous),
        out_specs=[
            pl.BlockSpec((1, tok_rows, step_heads * HD), lambda step: (0, 0, offset + step))
        ]
        * count,
        out_shape=[jax.ShapeDtypeStruct((1, tok_rows, width), jnp.bfloat16)] * count,
        input_output_aliases={1 + j: j for j in range(len(previous))},
        compiler_params=pltpu.CompilerParams(vmem_limit_bytes=16 * 1024 * 1024),
        name="unpack_heads",
    )(returned, *previous)


def on_device(queries, key_rows, value_rows, out_grad, prev_grads):
    arrays = (queries, key_rows, value_rows, out_grad)
    width = queries.shape[2]
    uly_count = lax.axis_size("uly")
    own_heads = width // uly_count // HD
    step_heads = math.gcd(4, uly_count)
    grad_sum = lax.psum_scatter(prev_grads[0], "dp", scatter_dimension=0, tiled=True)
    outputs = ()
    results = []
    for turn in range(own_heads):
        packed = pack_heads(arrays, turn * uly_count, uly_count, step_heads)
        arrived = lax.all_to_all(packed, "uly", split_axis=0, concat_axis=0, tiled=True)
        results.append(attend_head(arrived))
    results[-1], grad_sum = lax.optimization_barrier((results[-1], grad_sum))
    for turn in range(own_heads):
        returned = lax.all_to_all(results[turn], "uly", split_axis=0, concat_axis=0, tiled=True)
        outputs = unpack_heads(returned, outputs, turn * uly_count, width, step_heads)
    return (*outputs, grad_sum.astype(jnp.float32))


def solution(mesh):
    return jax.shard_map(
        on_device,
        mesh=mesh,
        in_specs=(
            P("dp", "uly", None),
            P("dp", "uly", None),
            P("dp", "uly", None),
            P("dp", "uly", None),
            P("dp", None, "uly"),
        ),
        out_specs=(
            P("dp", "uly", None),
            P("dp", "uly", None),
            P("dp", "uly", None),
            P("dp", "uly", None),
            P("dp", "uly"),
        ),
        check_vma=False,
    )
```

time: 541 us -> 247 us (0.46)
  matrix products: 226 us -> 0 us
  waiting for transfers between devices: 208 us -> 155 us
  Pallas kernels: 0 us -> 47.5 us
  local copies, waits for them, and re-layouts: 39.6 us -> 5.59 us
  starting transfers between devices: 44.1 us -> 23.7 us
    dot_general x20 -> x0, matrix products: 199 us -> none  [the longest x4 75.3 us: one_block(): jnp.einsum('hqk,qhd->khd', dscores, query_tile, preferred_element_type=jn...]
    pallas_call x0 -> x6, Pallas kernels: none -> 47.5 us  [the longest x2 35.7 us: attend_head(): pl.pallas_call(functools.partial(attend_body, block_chunks), grid=(chunks...]
    all_to_all x8 -> x4, waiting for transfers between devices: 180 us -> 135 us  [the longest x2 83.8 us: on_device(): lax.all_to_all(packed, 'uly', split_axis=0, concat_axis=0, tiled=True)]
    sub x4 -> x0, matrix products: 27.1 us -> none  [one_block(): shifted = jnp.exp(scores - row_max)]
    all_to_all x8 -> x4, starting transfers between devices: 44 us -> 23.6 us  [the longest x2 13.3 us: on_device(): lax.all_to_all(packed, 'uly', split_axis=0, concat_axis=0, tiled=True)]
    another operation x4 -> x0, local copies, waits for them, and re-layouts: 10.8 us -> none  [the longest x1 3.62 us: on_device(): qgrad_heads[:, None]]
    all_to_all x10 -> x0, local copies, waits for them, and re-layouts: 10.5 us -> none  [the longest x2 2.73 us: on_device(): lax.all_to_all(out_heads[:, None], 'uly', split_axis=0, concat_axis=1, ti...]
    unnamed x10, local copies, waits for them, and re-layouts: 15 us -> 5.59 us
  transfers between devices with their start and end apart: 9 -> 5, of which waited for: 9 -> 5; matrix products, arithmetic and copies ran while one was open for 7% -> 0% of each run, Pallas kernels for 0% -> 17%
where the time goes in v1:
time: 247 us
  waiting for transfers between devices  155 us (63%)
  Pallas kernels  47.5 us (19%)
  starting transfers between devices  23.7 us (10%)
  between operations  14 us (6%)
  local copies, waits for them, and re-layouts  5.59 us (2%)
    all_to_all x2, waiting for transfers between devices, on_device(): lax.all_to_all(packed, 'uly', split_axis=0, concat_axis=0, tiled=True)  83.8 us
    all_to_all x2, waiting for transfers between devices, on_device(): lax.all_to_all(results[turn], 'uly', split_axis=0, concat_axis=0, tiled=T...  51 us
    pallas_call x2, Pallas kernels, attend_head(): pl.pallas_call(functools.partial(attend_body, block_chunks), grid=(chunks...  35.7 us
    reduce_scatter x1, waiting for transfers between devices, on_device(): lax.psum_scatter(prev_grads[0], 'dp', scatter_dimension=0, tiled=True)  19.8 us
    all_to_all x2, starting transfers between devices, on_device(): lax.all_to_all(packed, 'uly', split_axis=0, concat_axis=0, tiled=True)  13.3 us
    all_to_all x2, starting transfers between devices, on_device(): lax.all_to_all(results[turn], 'uly', split_axis=0, concat_axis=0, tiled=T...  10.3 us
    pallas_call x2, Pallas kernels, pack_heads(): pl.pallas_call(pack_body, grid=(count // step_heads,), in_specs=[pl.Block...  7.93 us
    unnamed x10, local copies, waits for them, and re-layouts  5.59 us
  transfers between devices with their start and end apart: 5, of which 5 were waited for; matrix products, arithmetic and copies ran while one was open for 0% of the time, Pallas kernels for 17%

profile of v1, /device:TPU:64, one launch (start us, length us, event | category | flops | bytes accessed | tf_op | source)
XLA Modules:
  0.0 246.8 jit_solution(10489999970777972122)
XLA Ops:
  7.2 4.0 %pack_heads.3 = bf16[16,4,128,128]{3,2,1,0:T(8,128)(2,1)} custom-call(bf16[1,128,4096]{2,1,0:T(8,128)(2,1)} %refs_0_.3, bf16[1,128,4096]{2,1,0:T(8,128)(2,1)} %refs_1_.3, bf16[1,128,4096]{2,1,0:T(8,128)(2,1)} %refs_2_.3, bf16[1,128,4096]{2,1,0:T(8,128)(2,1)} %refs_3_.3), custom_call_target="tpu_custom_call" | custom-call | tf_op jit(solution)/shard_map/pack_heads/pallas_call | solution.py:101
  11.1 8.2 %all-to-all-start.2 = ((bf16[16,4,128,128]{3,2,1,0:T(8,128)(2,1)}), bf16[16,4,128,128]{3,2,1,0:T(8,128)(2,1)S(1)}, u32[]{:S(2)}, u32[]{:S(2)}) async-start(bf16[16,4,128,128]{3,2,1,0:T(8,128)(2,1)} %pack_heads.3), calls=%async_computation.3 | async-start | bytes 4194304 | tf_op jit(solution)/shard_map/all_to_all | solution.py:155
  19.3 4.0 %pack_heads.2 = bf16[16,4,128,128]{3,2,1,0:T(8,128)(2,1)} custom-call(bf16[1,128,4096]{2,1,0:T(8,128)(2,1)} %refs_0_.3, bf16[1,128,4096]{2,1,0:T(8,128)(2,1)} %refs_1_.3, bf16[1,128,4096]{2,1,0:T(8,128)(2,1)} %refs_2_.3, bf16[1,128,4096]{2,1,0:T(8,128)(2,1)} %refs_3_.3), custom_call_target="tpu_custom_call" | custom-call | tf_op jit(solution)/shard_map/pack_heads/pallas_call | solution.py:101
  23.3 44.3 %all-to-all-done.2.in_ref = bf16[16,4,128,128]{3,2,1,0:T(8,128)(2,1)S(1)} async-done(((bf16[16,4,128,128]{3,2,1,0:T(8,128)(2,1)}), bf16[16,4,128,128]{3,2,1,0:T(8,128)(2,1)S(1)}, u32[]{:S(2)}, u32[]{:S(2)}) %all-to-all-start.2) | async-done | bytes 2097184 | tf_op jit(solution)/shard_map/all_to_all | solution.py:155
  67.6 0.0 copy-start.3
  67.6 1.3 copy-done.3
  68.9 5.1 %all-to-all-start = ((bf16[16,4,128,128]{3,2,1,0:T(8,128)(2,1)}), bf16[16,4,128,128]{3,2,1,0:T(8,128)(2,1)S(1)}, u32[]{:S(2)}, u32[]{:S(2)}) async-start(bf16[16,4,128,128]{3,2,1,0:T(8,128)(2,1)} %pack_heads.2), calls=%async_computation | async-start | bytes 4194304 | tf_op jit(solution)/shard_map/all_to_all | solution.py:155
  74.1 0.0 reduce-scatter.2.cloned.1.call-start
  74.1 0.7 reduce-scatter.2.cloned.1.call-update
  74.8 17.8 %attend_head.3 = bf16[16,4,128,128]{3,2,1,0:T(8,128)(2,1)} custom-call(bf16[16,4,128,128]{3,2,1,0:T(8,128)(2,1)} %copy-done.3), custom_call_target="tpu_custom_call" | custom-call | flops 6442450944 | bytes 4194304 | tf_op jit(solution)/shard_map/attend_head/pallas_call | solution.py:71
  92.6 39.5 %all-to-all-done.in_ref = bf16[16,4,128,128]{3,2,1,0:T(8,128)(2,1)S(1)} async-done(((bf16[16,4,128,128]{3,2,1,0:T(8,128)(2,1)}), bf16[16,4,128,128]{3,2,1,0:T(8,128)(2,1)S(1)}, u32[]{:S(2)}, u32[]{:S(2)}) %all-to-all-start) | async-done | bytes 2097184 | tf_op jit(solution)/shard_map/all_to_all | solution.py:155
  132.1 1.3 copy-done.2
  133.5 4.2 %all-to-all-start.3 = ((bf16[16,4,128,128]{3,2,1,0:T(8,128)(2,1)}), bf16[16,4,128,128]{3,2,1,0:T(8,128)(2,1)S(1)}, u32[]{:S(2)}, u32[]{:S(2)}) async-start(bf16[16,4,128,128]{3,2,1,0:T(8,128)(2,1)} %attend_head.3), calls=%async_computation.4 | async-start | bytes 4194304 | tf_op jit(solution)/shard_map/all_to_all | solution.py:159
  137.7 17.9 %attend_head.2 = bf16[16,4,128,128]{3,2,1,0:T(8,128)(2,1)} custom-call(bf16[16,4,128,128]{3,2,1,0:T(8,128)(2,1)} %copy-done.2), custom_call_target="tpu_custom_call" | custom-call | flops 6442450944 | bytes 4194304 | tf_op jit(solution)/shard_map/attend_head/pallas_call | solution.py:71
  155.6 19.8 %reduce-scatter.2.cloned.1.call-done = bf16[320,256]{1,0:T(8,128)(2,1)} async-done(((bf16[5120,256]{1,0:T(8,128)(2,1)}), bf16[320,256]{1,0:T(8,128)(2,1)}) %reduce-scatter.2.cloned.1.call-update) | async-done | bytes 163856 | tf_op jit(solution)/shard_map/reduce_scatter | solution.py:150
  175.4 8.5 %all-to-all-done.3.in_ref = bf16[16,4,128,128]{3,2,1,0:T(8,128)(2,1)S(1)} async-done(((bf16[16,4,128,128]{3,2,1,0:T(8,128)(2,1)}), bf16[16,4,128,128]{3,2,1,0:T(8,128)(2,1)S(1)}, u32[]{:S(2)}, u32[]{:S(2)}) %all-to-all-start.3) | async-done | bytes 2097184 | tf_op jit(solution)/shard_map/all_to_all | solution.py:159
  183.9 1.3 copy-done
  185.2 6.1 %all-to-all-start.1 = ((bf16[16,4,128,128]{3,2,1,0:T(8,128)(2,1)}), bf16[16,4,128,128]{3,2,1,0:T(8,128)(2,1)S(1)}, u32[]{:S(2)}, u32[]{:S(2)}) async-start(bf16[16,4,128,128]{3,2,1,0:T(8,128)(2,1)} %attend_head.2), calls=%async_computation.2 | async-start | bytes 4194304 | tf_op jit(solution)/shard_map/all_to_all | solution.py:159
  191.3 0.0 copy-done.4
  191.3 0.7 convert_element_type.3
  192.0 1.6 copy-done.1
  193.6 1.9 unpack_heads.2
  195.5 42.5 %all-to-all-done.1.in_ref = bf16[16,4,128,128]{3,2,1,0:T(8,128)(2,1)S(1)} async-done(((bf16[16,4,128,128]{3,2,1,0:T(8,128)(2,1)}), bf16[16,4,128,128]{3,2,1,0:T(8,128)(2,1)S(1)}, u32[]{:S(2)}, u32[]{:S(2)}) %all-to-all-start.1) | async-done | bytes 2097184 | tf_op jit(solution)/shard_map/all_to_all | solution.py:159
  238.0 1.9 unpack_heads.3
  (4 shorter events, 0.0 us)
Async XLA Ops:
  11.1 56.5 %all-to-all-start.2 = ((bf16[16,4,128,128]{3,2,1,0:T(8,128)(2,1)}), bf16[16,4,128,128]{3,2,1,0:T(8,128)(2,1)S(1)}, u32[]{:S(2)}, u32[]{:S(2)}) async-start(bf16[16,4,128,128]{3,2,1,0:T(8,128)(2,1)} %pack_heads.3), calls=%async_computation.3 | async-start | bytes 4194304 | tf_op jit(solution)/shard_map/all_to_all | solution.py:155
  67.6 1.3 copy-start.3
  68.9 63.2 %all-to-all-start = ((bf16[16,4,128,128]{3,2,1,0:T(8,128)(2,1)}), bf16[16,4,128,128]{3,2,1,0:T(8,128)(2,1)S(1)}, u32[]{:S(2)}, u32[]{:S(2)}) async-start(bf16[16,4,128,128]{3,2,1,0:T(8,128)(2,1)} %pack_heads.2), calls=%async_computation | async-start | bytes 4194304 | tf_op jit(solution)/shard_map/all_to_all | solution.py:155
  74.1 101.3 %reduce-scatter.2.cloned.1.call-start = ((), (), s32[]{:S(2)}) async-start(), calls=%async_computation.5 | async-start | bytes 2785280 | tf_op jit(solution)/shard_map/reduce_scatter | solution.py:150
  132.1 1.3 copy-start.2
  133.5 50.4 %all-to-all-start.3 = ((bf16[16,4,128,128]{3,2,1,0:T(8,128)(2,1)}), bf16[16,4,128,128]{3,2,1,0:T(8,128)(2,1)S(1)}, u32[]{:S(2)}, u32[]{:S(2)}) async-start(bf16[16,4,128,128]{3,2,1,0:T(8,128)(2,1)} %attend_head.3), calls=%async_computation.4 | async-start | bytes 4194304 | tf_op jit(solution)/shard_map/all_to_all | solution.py:159
  175.4 15.9 %copy-start.4 = (bf16[320,256]{1,0:T(8,128)(2,1)S(1)}, bf16[320,256]{1,0:T(8,128)(2,1)}, u32[]{:S(2)}) copy-start(bf16[320,256]{1,0:T(8,128)(2,1)} %reduce-scatter.2.cloned.1.call-done) | copy-start | bytes 491524
  183.9 1.3 copy-start
  185.2 52.9 %all-to-all-start.1 = ((bf16[16,4,128,128]{3,2,1,0:T(8,128)(2,1)}), bf16[16,4,128,128]{3,2,1,0:T(8,128)(2,1)S(1)}, u32[]{:S(2)}, u32[]{:S(2)}) async-start(bf16[16,4,128,128]{3,2,1,0:T(8,128)(2,1)} %attend_head.2), calls=%async_computation.2 | async-start | bytes 4194304 | tf_op jit(solution)/shard_map/all_to_all | solution.py:159
  192.0 1.6 copy-start.1
Sparse Core Ops, SparseCore 0:
  79.2 96.1 reduce-scatter.1

commit v2 on v1

--- a/solution.py
+++ b/solution.py
@@ -136,9 +136,39 @@
         * count,
         out_shape=[jax.ShapeDtypeStruct((1, tok_rows, width), jnp.bfloat16)] * count,
         input_output_aliases={1 + j: j for j in range(len(previous))},
-        compiler_params=pltpu.CompilerParams(vmem_limit_bytes=16 * 1024 * 1024),
+        compiler_params=pltpu.CompilerParams(vmem_limit_bytes=60 * 1024 * 1024),
         name="unpack_heads",
     )(returned, *previous)
+
+
+def half_terms(terms):
+    count = lax.axis_size("dp")
+    half = count // 2
+    place = lax.axis_index("dp") % half
+    rows = terms.shape[0] // half
+    parts = []
+    for s in range(half):
+        part = lax.dynamic_slice_in_dim(terms, (place ^ s) * rows, rows, 0)
+        if s:
+            part = lax.ppermute(part, "dp", [(a, a ^ s) for a in range(count)])
+        parts.append(part)
+    return parts
+
+
+def half_sums(parts):
+    total = sum(part.astype(jnp.float32) for part in parts)
+    return total.astype(parts[0].dtype).reshape(2, parts[0].shape[0] // 2, -1)
+
+
+def both_halves(sums):
+    half = lax.axis_size("dp") // 2
+    side = lax.axis_index("dp") // half
+    arrived = []
+    for flip in range(2):
+        block = lax.dynamic_index_in_dim(sums, side ^ flip, 0, keepdims=False)
+        pairs = [(h * half + a, 2 * a + (h ^ flip)) for h in range(2) for a in range(half)]
+        arrived.append(lax.ppermute(block, "dp", pairs))
+    return arrived
 
 
 def on_device(queries, key_rows, value_rows, out_grad, prev_grads):
@@ -146,19 +176,26 @@
     width = queries.shape[2]
     uly_count = lax.axis_size("uly")
     own_heads = width // uly_count // HD
-    step_heads = math.gcd(4, uly_count)
-    grad_sum = lax.psum_scatter(prev_grads[0], "dp", scatter_dimension=0, tiled=True)
+    step_heads = math.gcd(8, uly_count)
     outputs = ()
     results = []
     for turn in range(own_heads):
         packed = pack_heads(arrays, turn * uly_count, uly_count, step_heads)
+        if turn == 0:
+            packed, terms = lax.optimization_barrier((packed, prev_grads[0]))
+            parts = half_terms(terms)
+        else:
+            packed, *parts[1:3] = lax.optimization_barrier((packed, *parts[1:3]))
         arrived = lax.all_to_all(packed, "uly", split_axis=0, concat_axis=0, tiled=True)
         results.append(attend_head(arrived))
-    results[-1], grad_sum = lax.optimization_barrier((results[-1], grad_sum))
+    results[0], parts = lax.optimization_barrier((results[0], parts))
+    results[0], sums = lax.optimization_barrier((results[0], half_sums(parts)))
+    results[-1], arrived = lax.optimization_barrier((results[-1], both_halves(sums)))
+    grad_sum = arrived[0].astype(jnp.float32) + arrived[1].astype(jnp.float32)
     for turn in range(own_heads):
         returned = lax.all_to_all(results[turn], "uly", split_axis=0, concat_axis=0, tiled=True)
         outputs = unpack_heads(returned, outputs, turn * uly_count, width, step_heads)
-    return (*outputs, grad_sum.astype(jnp.float32))
+    return (*outputs, grad_sum)
 
 
 def solution(mesh):

time: 247 us -> 232 us (0.939)
  between operations: 14 us -> 0.68 us
  waiting for transfers between devices: 155 us -> 144 us
  starting transfers between devices: 23.7 us -> 32.6 us
    all_to_all x2, waiting for transfers between devices: 83.8 us -> 50.9 us  [on_device(): lax.all_to_all(packed, 'uly', split_axis=0, concat_axis=0, tiled=True)]
    ppermute x0 -> x9, waiting for transfers between devices: none -> 25.7 us  [the longest x7 13.6 us: half_terms(): part = lax.ppermute(part, 'dp', [(a, a ^ s) for a in range(count)])]
    reduce_scatter x1 -> x0, waiting for transfers between devices: 19.8 us -> none  [on_device(): lax.psum_scatter(prev_grads[0], 'dp', scatter_dimension=0, tiled=True)]
    all_to_all x2, waiting for transfers between devices: 51 us -> 67.1 us  [on_device(): lax.all_to_all(results[turn], 'uly', split_axis=0, concat_axis=0, tiled=T...]
    ppermute x0 -> x9, starting transfers between devices: none -> 8.65 us  [the longest x7 7.7 us: half_terms(): part = lax.ppermute(part, 'dp', [(a, a ^ s) for a in range(count)])]
    pallas_call x2, Pallas kernels: 7.93 us -> 5.41 us  [pack_heads(): pl.pallas_call(pack_body, grid=(count // step_heads,), in_specs=[pl.Block...]
  transfers between devices with their start and end apart: 5 -> 13, of which waited for: 5 -> 8; matrix products, arithmetic and copies ran while one was open for 0% -> 2% of each run, Pallas kernels for 17% -> 18%
where the time goes in v2:
time: 232 us; the launch traced here: 231 us
  waiting for transfers between devices  144 us (62%)
  Pallas kernels  46.7 us (20%)
  starting transfers between devices  32.6 us (14%)
  local copies, waits for them, and re-layouts  5.21 us (2%)
  other arithmetic  2.56 us (1%)
    all_to_all x2, waiting for transfers between devices, on_device(): lax.all_to_all(results[turn], 'uly', split_axis=0, concat_axis=0, tiled=T...  67.1 us
    all_to_all x2, waiting for transfers between devices, on_device(): lax.all_to_all(packed, 'uly', split_axis=0, concat_axis=0, tiled=True)  50.9 us
    pallas_call x2, Pallas kernels, attend_head(): pl.pallas_call(functools.partial(attend_body, block_chunks), grid=(chunks...  35.7 us
    all_to_all x2, starting transfers between devices, on_device(): lax.all_to_all(packed, 'uly', split_axis=0, concat_axis=0, tiled=True)  13.6 us
    ppermute x7, waiting for transfers between devices, half_terms(): part = lax.ppermute(part, 'dp', [(a, a ^ s) for a in range(count)])  13.6 us
    ppermute x2, waiting for transfers between devices, both_halves(): arrived.append(lax.ppermute(block, 'dp', pairs))  12.1 us
    all_to_all x2, starting transfers between devices, on_device(): lax.all_to_all(results[turn], 'uly', split_axis=0, concat_axis=0, tiled=T...  10.3 us
    ppermute x7, starting transfers between devices, half_terms(): part = lax.ppermute(part, 'dp', [(a, a ^ s) for a in range(count)])  7.7 us
  transfers between devices with their start and end apart: 13, of which 8 were waited for; matrix products, arithmetic and copies ran while one was open for 2% of the time, Pallas kernels for 18%

profile of v2, /device:TPU:64, one launch (start us, length us, event | category | flops | bytes accessed | tf_op | source)
XLA Modules:
  0.0 231.3 jit_solution(16344902973828166349)
XLA Ops:
  0.6 2.7 %pack_heads.3 = bf16[16,4,128,128]{3,2,1,0:T(8,128)(2,1)} custom-call(bf16[1,128,4096]{2,1,0:T(8,128)(2,1)} %refs_0_.3, bf16[1,128,4096]{2,1,0:T(8,128)(2,1)} %refs_1_.3, bf16[1,128,4096]{2,1,0:T(8,128)(2,1)} %refs_2_.3, bf16[1,128,4096]{2,1,0:T(8,128)(2,1)} %refs_3_.3), custom_call_target="tpu_custom_call" | custom-call | tf_op jit(solution)/shard_map/pack_heads/pallas_call | solution.py:101
  3.3 8.5 %all-to-all-start.1 = ((bf16[16,4,128,128]{3,2,1,0:T(8,128)(2,1)}), bf16[16,4,128,128]{3,2,1,0:T(8,128)(2,1)}, u32[]{:S(2)}, u32[]{:S(2)}) async-start(bf16[16,4,128,128]{3,2,1,0:T(8,128)(2,1)} %pack_heads.3), calls=%async_computation.1 | async-start | bytes 4194304 | tf_op jit(solution)/shard_map/all_to_all | solution.py:189
  13.0 1.5 collective-permute-start.1
  14.5 2.7 %pack_heads.2 = bf16[16,4,128,128]{3,2,1,0:T(8,128)(2,1)} custom-call(bf16[1,128,4096]{2,1,0:T(8,128)(2,1)} %refs_0_.3, bf16[1,128,4096]{2,1,0:T(8,128)(2,1)} %refs_1_.3, bf16[1,128,4096]{2,1,0:T(8,128)(2,1)} %refs_2_.3, bf16[1,128,4096]{2,1,0:T(8,128)(2,1)} %refs_3_.3), custom_call_target="tpu_custom_call" | custom-call | tf_op jit(solution)/shard_map/pack_heads/pallas_call | solution.py:101
  17.2 5.0 %collective-permute-done.1 = bf16[640,256]{1,0:T(8,128)(2,1)} collective-permute-done((bf16[640,256]{1,0:T(8,128)(2,1)}, bf16[640,256]{1,0:T(8,128)(2,1)}, u32[]{:S(2)}, u32[]{:S(2)}) %collective-permute-start.1) | collective-permute-done | bytes 327712 | tf_op jit(solution)/shard_map/ppermute | solution.py:153
  22.2 38.0 %all-to-all-done.1.in_ref = bf16[16,4,128,128]{3,2,1,0:T(8,128)(2,1)} async-done(((bf16[16,4,128,128]{3,2,1,0:T(8,128)(2,1)}), bf16[16,4,128,128]{3,2,1,0:T(8,128)(2,1)}, u32[]{:S(2)}, u32[]{:S(2)}) %all-to-all-start.1) | async-done | bytes 2097184 | tf_op jit(solution)/shard_map/all_to_all | solution.py:189
  60.2 5.1 %all-to-all-start = ((bf16[16,4,128,128]{3,2,1,0:T(8,128)(2,1)}), bf16[16,4,128,128]{3,2,1,0:T(8,128)(2,1)S(1)}, u32[]{:S(2)}, u32[]{:S(2)}) async-start(bf16[16,4,128,128]{3,2,1,0:T(8,128)(2,1)} %pack_heads.2), calls=%async_computation | async-start | bytes 4194304 | tf_op jit(solution)/shard_map/all_to_all | solution.py:189
  66.0 2.1 collective-permute-start.5
  68.1 1.6 collective-permute-start.4
  69.8 1.7 collective-permute-start.3
  71.5 17.8 %attend_head.3 = bf16[16,4,128,128]{3,2,1,0:T(8,128)(2,1)} custom-call(bf16[16,4,128,128]{3,2,1,0:T(8,128)(2,1)} %all-to-all-done.1.in_ref), custom_call_target="tpu_custom_call" | custom-call | flops 6442450944 | bytes 4194304 | tf_op jit(solution)/shard_map/attend_head/pallas_call | solution.py:71
  89.3 1.3 collective-permute-done.6
  90.7 7.2 %collective-permute-done.5 = bf16[640,256]{1,0:T(8,128)(2,1)} collective-permute-done((bf16[640,256]{1,0:T(8,128)(2,1)}, bf16[640,256]{1,0:T(8,128)(2,1)}, u32[]{:S(2)}, u32[]{:S(2)}) %collective-permute-start.5) | collective-permute-done | bytes 327712 | tf_op jit(solution)/shard_map/ppermute | solution.py:153
  97.9 1.8 add_convert_fusion
  99.7 12.9 %all-to-all-done.in_ref = bf16[16,4,128,128]{3,2,1,0:T(8,128)(2,1)S(1)} async-done(((bf16[16,4,128,128]{3,2,1,0:T(8,128)(2,1)}), bf16[16,4,128,128]{3,2,1,0:T(8,128)(2,1)S(1)}, u32[]{:S(2)}, u32[]{:S(2)}) %all-to-all-start) | async-done | bytes 2097184 | tf_op jit(solution)/shard_map/all_to_all | solution.py:189
  112.6 1.3 copy-done.3
  113.9 5.2 %all-to-all-start.3 = ((bf16[16,4,128,128]{3,2,1,0:T(8,128)(2,1)}), bf16[16,4,128,128]{3,2,1,0:T(8,128)(2,1)S(1)}, u32[]{:S(2)}, u32[]{:S(2)}) async-start(bf16[16,4,128,128]{3,2,1,0:T(8,128)(2,1)} %attend_head.3), calls=%async_computation.3 | async-start | bytes 4194304 | tf_op jit(solution)/shard_map/all_to_all | solution.py:196
  120.1 17.9 %attend_head.2 = bf16[16,4,128,128]{3,2,1,0:T(8,128)(2,1)} custom-call(bf16[16,4,128,128]{3,2,1,0:T(8,128)(2,1)} %copy-done.3), custom_call_target="tpu_custom_call" | custom-call | flops 6442450944 | bytes 4194304 | tf_op jit(solution)/shard_map/attend_head/pallas_call | solution.py:71
  138.0 12.1 %collective-permute-done.8 = bf16[320,256]{1,0:T(8,128)(2,1)S(1)} collective-permute-done((bf16[320,256]{1,0:T(8,128)(2,1)S(1)}, bf16[320,256]{1,0:T(8,128)(2,1)S(1)}, u32[]{:S(2)}, u32[]{:S(2)}) %collective-permute-start.8) | collective-permute-done | bytes 163872 | tf_op jit(solution)/shard_map/ppermute | solution.py:170
  150.1 23.4 %all-to-all-done.3.in_ref = bf16[16,4,128,128]{3,2,1,0:T(8,128)(2,1)S(1)} async-done(((bf16[16,4,128,128]{3,2,1,0:T(8,128)(2,1)}), bf16[16,4,128,128]{3,2,1,0:T(8,128)(2,1)S(1)}, u32[]{:S(2)}, u32[]{:S(2)}) %all-to-all-start.3) | async-done | bytes 2097184 | tf_op jit(solution)/shard_map/all_to_all | solution.py:196
  174.7 5.2 %all-to-all-start.2 = ((bf16[16,4,128,128]{3,2,1,0:T(8,128)(2,1)}), bf16[16,4,128,128]{3,2,1,0:T(8,128)(2,1)S(1)}, u32[]{:S(2)}, u32[]{:S(2)}) async-start(bf16[16,4,128,128]{3,2,1,0:T(8,128)(2,1)} %attend_head.2), calls=%async_computation.2 | async-start | bytes 4194304 | tf_op jit(solution)/shard_map/all_to_all | solution.py:196
  180.6 2.8 %unpack_heads.2 = (bf16[1,128,4096]{2,1,0:T(8,128)(2,1)}, bf16[1,128,4096]{2,1,0:T(8,128)(2,1)}, bf16[1,128,4096]{2,1,0:T(8,128)(2,1)}, bf16[1,128,4096]{2,1,0:T(8,128)(2,1)}) custom-call(bf16[16,4,128,128]{3,2,1,0:T(8,128)(2,1)} %copy-done.1), custom_call_target="tpu_custom_call" | custom-call | tf_op jit(solution)/shard_map/unpack_heads/pallas_call | solution.py:126
  183.5 43.7 %all-to-all-done.2.in_ref = bf16[16,4,128,128]{3,2,1,0:T(8,128)(2,1)S(1)} async-done(((bf16[16,4,128,128]{3,2,1,0:T(8,128)(2,1)}), bf16[16,4,128,128]{3,2,1,0:T(8,128)(2,1)S(1)}, u32[]{:S(2)}, u32[]{:S(2)}) %all-to-all-start.2) | async-done | bytes 2097184 | tf_op jit(solution)/shard_map/all_to_all | solution.py:196
  228.5 2.8 %unpack_heads.3 = (bf16[1,128,4096]{2,1,0:T(8,128)(2,1)}, bf16[1,128,4096]{2,1,0:T(8,128)(2,1)}, bf16[1,128,4096]{2,1,0:T(8,128)(2,1)}, bf16[1,128,4096]{2,1,0:T(8,128)(2,1)}) custom-call(bf16[16,4,128,128]{3,2,1,0:T(8,128)(2,1)} %copy-done, ...), custom_call_target="tpu_custom_call", output_to_operand_aliasing={{0}: (1, {}), {1}: (2, {}), {2}: (3, {}), {3}: (4, {})} | custom-call | tf_op jit(solution)/shard_map/unpack_heads/pallas_call | solution.py:126
  (22 shorter events, 6.3 us)
Async XLA Ops:
  3.3 8.5 %copy-start.2 = (bf16[1,5120,256]{2,1,0:T(8,128)(2,1)S(1)}, bf16[1,5120,256]{2,1,0:T(8,128)(2,1)}, u32[]{:S(2)}) copy-start(bf16[1,5120,256]{2,1,0:T(8,128)(2,1)} %param.9) | copy-start | bytes 7864324
  3.3 56.8 %all-to-all-start.1 = ((bf16[16,4,128,128]{3,2,1,0:T(8,128)(2,1)}), bf16[16,4,128,128]{3,2,1,0:T(8,128)(2,1)}, u32[]{:S(2)}, u32[]{:S(2)}) async-start(bf16[16,4,128,128]{3,2,1,0:T(8,128)(2,1)} %pack_heads.3), calls=%async_computation.1 | async-start | bytes 4194304 | tf_op jit(solution)/shard_map/all_to_all | solution.py:189
  13.0 9.2 %collective-permute-start.1 = (bf16[640,256]{1,0:T(8,128)(2,1)}, bf16[640,256]{1,0:T(8,128)(2,1)}, u32[]{:S(2)}, u32[]{:S(2)}) collective-permute-start(bf16[640,256]{1,0:T(8,128)(2,1)} %get-tuple-element.65), channel_id=1, source_target_pairs={{0,32},{16,48},{32,0},{48,16},{64,96},{80,112},{96,64},{112,80},{1... | collective-permute-start | bytes 983048 | tf_op jit(solution)/shard_map/ppermute | solution.py:153
  14.5 7.7 %collective-permute-start = (bf16[640,256]{1,0:T(8,128)(2,1)S(1)}, bf16[640,256]{1,0:T(8,128)(2,1)}, u32[]{:S(2)}, u32[]{:S(2)}) collective-permute-start(bf16[640,256]{1,0:T(8,128)(2,1)S(1)} %get-tuple-element.66), channel_id=1, source_target_pairs={{0,16},{16,0},{32,48},{48,32},{64,80},{80,64},{96,112},{112,96},{1... | collective-permute-start | bytes 983048 | tf_op jit(solution)/shard_map/ppermute | solution.py:153
  17.2 52.6 %copy-start.4 = (bf16[640,256]{1,0:T(8,128)(2,1)S(1)}, bf16[640,256]{1,0:T(8,128)(2,1)}, u32[]{:S(2)}) copy-start(bf16[640,256]{1,0:T(8,128)(2,1)} %get-tuple-element.62) | copy-start | bytes 983044
  60.2 52.4 %all-to-all-start = ((bf16[16,4,128,128]{3,2,1,0:T(8,128)(2,1)}), bf16[16,4,128,128]{3,2,1,0:T(8,128)(2,1)S(1)}, u32[]{:S(2)}, u32[]{:S(2)}) async-start(bf16[16,4,128,128]{3,2,1,0:T(8,128)(2,1)} %pack_heads.2), calls=%async_computation | async-start | bytes 4194304 | tf_op jit(solution)/shard_map/all_to_all | solution.py:189
  65.3 25.4 %collective-permute-start.6 = (bf16[640,256]{1,0:T(8,128)(2,1)}, bf16[640,256]{1,0:T(8,128)(2,1)S(1)}, u32[]{:S(2)}, u32[]{:S(2)}) collective-permute-start(bf16[640,256]{1,0:T(8,128)(2,1)} %get-tuple-element.59), channel_id=1, source_target_pairs={{0,112},{16,96},{32,80},{48,64},{64,48},{80,32},{96,16},{112,0},{1... | collective-permute-start | bytes 983048 | tf_op jit(solution)/shard_map/ppermute | solution.py:153
  66.0 31.9 %collective-permute-start.5 = (bf16[640,256]{1,0:T(8,128)(2,1)}, bf16[640,256]{1,0:T(8,128)(2,1)}, u32[]{:S(2)}, u32[]{:S(2)}) collective-permute-start(bf16[640,256]{1,0:T(8,128)(2,1)} %get-tuple-element.60), channel_id=1, source_target_pairs={{0,96},{16,112},{32,64},{48,80},{64,32},{80,48},{96,0},{112,16},{1... | collective-permute-start | bytes 983048 | tf_op jit(solution)/shard_map/ppermute | solution.py:153
  68.1 29.8 %collective-permute-start.4 = (bf16[640,256]{1,0:T(8,128)(2,1)}, bf16[640,256]{1,0:T(8,128)(2,1)}, u32[]{:S(2)}, u32[]{:S(2)}) collective-permute-start(bf16[640,256]{1,0:T(8,128)(2,1)} %get-tuple-element.61), channel_id=1, source_target_pairs={{0,80},{16,64},{32,112},{48,96},{64,16},{80,0},{96,48},{112,32},{1... | collective-permute-start | bytes 983048 | tf_op jit(solution)/shard_map/ppermute | solution.py:153
  69.8 28.1 %collective-permute-start.3 = (bf16[640,256]{1,0:T(8,128)(2,1)S(1)}, bf16[640,256]{1,0:T(8,128)(2,1)}, u32[]{:S(2)}, u32[]{:S(2)}) collective-permute-start(bf16[640,256]{1,0:T(8,128)(2,1)S(1)} %copy-done.4), channel_id=1, source_target_pairs={{0,64},{16,80},{32,96},{48,112},{64,0},{80,16},{96,32},{112,48},{1... | collective-permute-start | bytes 983048 | tf_op jit(solution)/shard_map/ppermute | solution.py:153
  71.5 26.4 %collective-permute-start.2 = (bf16[640,256]{1,0:T(8,128)(2,1)S(1)}, bf16[640,256]{1,0:T(8,128)(2,1)}, u32[]{:S(2)}, u32[]{:S(2)}) collective-permute-start(bf16[640,256]{1,0:T(8,128)(2,1)S(1)} %get-tuple-element.63), channel_id=1, source_target_pairs={{0,48},{16,32},{32,16},{48,0},{64,112},{80,96},{96,80},{112,64},{1... | collective-permute-start | bytes 983048 | tf_op jit(solution)/shard_map/ppermute | solution.py:153
  112.6 1.3 copy-start.3
  113.9 59.5 %all-to-all-start.3 = ((bf16[16,4,128,128]{3,2,1,0:T(8,128)(2,1)}), bf16[16,4,128,128]{3,2,1,0:T(8,128)(2,1)S(1)}, u32[]{:S(2)}, u32[]{:S(2)}) async-start(bf16[16,4,128,128]{3,2,1,0:T(8,128)(2,1)} %attend_head.3), calls=%async_computation.3 | async-start | bytes 4194304 | tf_op jit(solution)/shard_map/all_to_all | solution.py:196
  119.1 30.9 %collective-permute-start.8 = (bf16[320,256]{1,0:T(8,128)(2,1)S(1)}, bf16[320,256]{1,0:T(8,128)(2,1)S(1)}, u32[]{:S(2)}, u32[]{:S(2)}) collective-permute-start(bf16[320,256]{1,0:T(8,128)(2,1)S(1)} %get-tuple-element.67), channel_id=1, source_target_pairs={{0,16},{16,48},{32,80},{48,112},{64,144},{80,176},{96,208},{112,24... | collective-permute-start | bytes 491528 | tf_op jit(solution)/shard_map/ppermute | solution.py:170
  119.2 30.8 %collective-permute-start.7 = (bf16[320,256]{1,0:T(8,128)(2,1)S(1)}, bf16[320,256]{1,0:T(8,128)(2,1)S(1)}, u32[]{:S(2)}, u32[]{:S(2)}) collective-permute-start(bf16[320,256]{1,0:T(8,128)(2,1)S(1)} %get-tuple-element.68), channel_id=1, source_target_pairs={{0,0},{16,32},{32,64},{48,96},{64,128},{80,160},{96,192},{112,224}... | collective-permute-start | bytes 491528 | tf_op jit(solution)/shard_map/ppermute | solution.py:170
  173.4 1.3 copy-start.1
  174.7 52.5 %all-to-all-start.2 = ((bf16[16,4,128,128]{3,2,1,0:T(8,128)(2,1)}), bf16[16,4,128,128]{3,2,1,0:T(8,128)(2,1)S(1)}, u32[]{:S(2)}, u32[]{:S(2)}) async-start(bf16[16,4,128,128]{3,2,1,0:T(8,128)(2,1)} %attend_head.2), calls=%async_computation.2 | async-start | bytes 4194304 | tf_op jit(solution)/shard_map/all_to_all | solution.py:196
  227.2 1.3 copy-start

commit v3 on v2

--- a/solution.py
+++ b/solution.py
@@ -78,7 +78,7 @@
             pltpu.VMEM((HD, seq_len), jnp.float32),
             pltpu.VMEM((HD, seq_len), jnp.float32),
         ],
-        compiler_params=pltpu.CompilerParams(vmem_limit_bytes=60 * 1024 * 1024),
+        compiler_params=pltpu.CompilerParams(vmem_limit_bytes=44 * 1024 * 1024),
         cost_estimate=pl.CostEstimate(
             flops=12 * seq_len * seq_len * HD,
             bytes_accessed=4 * packed.size,
@@ -120,7 +120,7 @@
             out_ref[0, :, source * HD : (source + 1) * HD] = in_ref[source, j]
 
 
-def unpack_heads(returned, previous, first, width, step_heads):
+def unpack_heads(returned, previous, first, width, step_heads, vmem_mib):
     heads, count, tok_rows, _ = returned.shape
     offset = first // step_heads
     return pl.pallas_call(
@@ -136,7 +136,7 @@
         * count,
         out_shape=[jax.ShapeDtypeStruct((1, tok_rows, width), jnp.bfloat16)] * count,
         input_output_aliases={1 + j: j for j in range(len(previous))},
-        compiler_params=pltpu.CompilerParams(vmem_limit_bytes=60 * 1024 * 1024),
+        compiler_params=pltpu.CompilerParams(vmem_limit_bytes=vmem_mib * 1024 * 1024),
         name="unpack_heads",
     )(returned, *previous)
 
@@ -194,7 +194,10 @@
     grad_sum = arrived[0].astype(jnp.float32) + arrived[1].astype(jnp.float32)
     for turn in range(own_heads):
         returned = lax.all_to_all(results[turn], "uly", split_axis=0, concat_axis=0, tiled=True)
-        outputs = unpack_heads(returned, outputs, turn * uly_count, width, step_heads)
+        vmem_mib = 16 if turn == own_heads - 1 else 60
+        outputs = unpack_heads(
+            returned, outputs, turn * uly_count, width, step_heads, vmem_mib
+        )
     return (*outputs, grad_sum)
 
 

time: 232 us -> 226 us (0.974)
  Pallas kernels: 46.7 us -> 42.6 us
    pallas_call x2, Pallas kernels: 35.7 us -> 32.8 us  [attend_head(): pl.pallas_call(functools.partial(attend_body, block_chunks), grid=(chunks...]
    unnamed x10 -> x2, local copies, waits for them, and re-layouts: 3.99 us -> 1.3 us
  transfers between devices with their start and end apart: 13 -> 13, of which waited for: 8 -> 8; matrix products, arithmetic and copies ran while one was open for 2% -> 2% of each run, Pallas kernels for 18% -> 17%
where the time goes in v3:
time: 226 us
  waiting for transfers between devices  144 us (64%)
  Pallas kernels  42.6 us (19%)
  starting transfers between devices  32.3 us (14%)
  local copies, waits for them, and re-layouts  3.99 us (2%)
    all_to_all x2, waiting for transfers between devices, on_device(): lax.all_to_all(results[turn], 'uly', split_axis=0, concat_axis=0, tiled=T...  67.2 us
    all_to_all x2, waiting for transfers between devices, on_device(): lax.all_to_all(packed, 'uly', split_axis=0, concat_axis=0, tiled=True)  49.9 us
    pallas_call x2, Pallas kernels, attend_head(): pl.pallas_call(functools.partial(attend_body, block_chunks), grid=(chunks...  32.8 us
    ppermute x7, waiting for transfers between devices, half_terms(): part = lax.ppermute(part, 'dp', [(a, a ^ s) for a in range(count)])  15 us
    all_to_all x2, starting transfers between devices, on_device(): lax.all_to_all(packed, 'uly', split_axis=0, concat_axis=0, tiled=True)  13.3 us
    ppermute x2, waiting for transfers between devices, both_halves(): arrived.append(lax.ppermute(block, 'dp', pairs))  12.1 us
    all_to_all x2, starting transfers between devices, on_device(): lax.all_to_all(results[turn], 'uly', split_axis=0, concat_axis=0, tiled=T...  10.3 us
    ppermute x7, starting transfers between devices, half_terms(): part = lax.ppermute(part, 'dp', [(a, a ^ s) for a in range(count)])  7.7 us
  transfers between devices with their start and end apart: 13, of which 8 were waited for; matrix products, arithmetic and copies ran while one was open for 2% of the time, Pallas kernels for 17%

profile of v3, /device:TPU:64, one launch (start us, length us, event | category | flops | bytes accessed | tf_op | source)
XLA Modules:
  0.0 226.0 jit_solution(14737765842768724971)
XLA Ops:
  0.6 2.7 %pack_heads.3 = bf16[16,4,128,128]{3,2,1,0:T(8,128)(2,1)} custom-call(bf16[1,128,4096]{2,1,0:T(8,128)(2,1)} %refs_0_.3, bf16[1,128,4096]{2,1,0:T(8,128)(2,1)} %refs_1_.3, bf16[1,128,4096]{2,1,0:T(8,128)(2,1)} %refs_2_.3, bf16[1,128,4096]{2,1,0:T(8,128)(2,1)} %refs_3_.3), custom_call_target="tpu_custom_call" | custom-call | tf_op jit(solution)/shard_map/pack_heads/pallas_call | solution.py:101
  3.4 8.2 %all-to-all-start.1 = ((bf16[16,4,128,128]{3,2,1,0:T(8,128)(2,1)}), bf16[16,4,128,128]{3,2,1,0:T(8,128)(2,1)S(1)}, u32[]{:S(2)}, u32[]{:S(2)}) async-start(bf16[16,4,128,128]{3,2,1,0:T(8,128)(2,1)} %pack_heads.3), calls=%async_computation.1 | async-start | bytes 4194304 | tf_op jit(solution)/shard_map/all_to_all | solution.py:189
  11.6 2.7 %constant_dynamic-slice_fusion = (bf16[640,256]{1,0:T(8,128)(2,1)}, bf16[640,256]{1,0:T(8,128)(2,1)}, bf16[640,256]{1,0:T(8,128)(2,1)S(1)}, bf16[640,256]{1,0:T(...) fusion(bf16[5120,256]{1,0:T(8,128)(2,1)} %bitcast.6, ...), kind=kLoop, calls=%fused_computation.4 | loop fusion | bytes 5242912 | tf_op jit(solution)/shard_map/dynamic_slice | solution.py:151
  14.2 1.5 collective-permute-start.1
  15.7 2.7 %pack_heads.2 = bf16[16,4,128,128]{3,2,1,0:T(8,128)(2,1)} custom-call(bf16[1,128,4096]{2,1,0:T(8,128)(2,1)} %refs_0_.3, bf16[1,128,4096]{2,1,0:T(8,128)(2,1)} %refs_1_.3, bf16[1,128,4096]{2,1,0:T(8,128)(2,1)} %refs_2_.3, bf16[1,128,4096]{2,1,0:T(8,128)(2,1)} %refs_3_.3), custom_call_target="tpu_custom_call" | custom-call | tf_op jit(solution)/shard_map/pack_heads/pallas_call | solution.py:101
  18.4 5.0 %collective-permute-done.1 = bf16[640,256]{1,0:T(8,128)(2,1)} collective-permute-done((bf16[640,256]{1,0:T(8,128)(2,1)}, bf16[640,256]{1,0:T(8,128)(2,1)}, u32[]{:S(2)}, u32[]{:S(2)}) %collective-permute-start.1) | collective-permute-done | bytes 327712 | tf_op jit(solution)/shard_map/ppermute | solution.py:153
  23.4 36.4 %all-to-all-done.1.in_ref = bf16[16,4,128,128]{3,2,1,0:T(8,128)(2,1)S(1)} async-done(((bf16[16,4,128,128]{3,2,1,0:T(8,128)(2,1)}), bf16[16,4,128,128]{3,2,1,0:T(8,128)(2,1)S(1)}, u32[]{:S(2)}, u32[]{:S(2)}) %all-to-all-start.1) | async-done | bytes 2097184 | tf_op jit(solution)/shard_map/all_to_all | solution.py:189
  59.8 5.1 %all-to-all-start = ((bf16[16,4,128,128]{3,2,1,0:T(8,128)(2,1)}), bf16[16,4,128,128]{3,2,1,0:T(8,128)(2,1)}, u32[]{:S(2)}, u32[]{:S(2)}) async-start(bf16[16,4,128,128]{3,2,1,0:T(8,128)(2,1)} %pack_heads.2), calls=%async_computation | async-start | bytes 4194304 | tf_op jit(solution)/shard_map/all_to_all | solution.py:189
  65.7 2.1 collective-permute-start.5
  67.8 1.6 collective-permute-start.4
  69.4 1.7 collective-permute-start.3
  71.2 16.2 %attend_head.3 = bf16[16,4,128,128]{3,2,1,0:T(8,128)(2,1)} custom-call(bf16[16,4,128,128]{3,2,1,0:T(8,128)(2,1)S(1)} %all-to-all-done.1.in_ref), custom_call_target="tpu_custom_call" | custom-call | flops 6442450944 | bytes 4194304 | tf_op jit(solution)/shard_map/attend_head/pallas_call | solution.py:71
  87.4 2.9 %collective-permute-done.6 = bf16[640,256]{1,0:T(8,128)(2,1)S(1)} collective-permute-done((bf16[640,256]{1,0:T(8,128)(2,1)}, bf16[640,256]{1,0:T(8,128)(2,1)S(1)}, u32[]{:S(2)}, u32[]{:S(2)}) %collective-permute-start.6) | collective-permute-done | bytes 327712 | tf_op jit(solution)/shard_map/ppermute | solution.py:153
  90.3 7.1 %collective-permute-done.5 = bf16[640,256]{1,0:T(8,128)(2,1)S(1)} collective-permute-done((bf16[640,256]{1,0:T(8,128)(2,1)}, bf16[640,256]{1,0:T(8,128)(2,1)S(1)}, u32[]{:S(2)}, u32[]{:S(2)}) %collective-permute-start.5) | collective-permute-done | bytes 327712 | tf_op jit(solution)/shard_map/ppermute | solution.py:153
  97.5 1.4 add_convert_fusion
  98.9 13.5 %all-to-all-done.in_ref = bf16[16,4,128,128]{3,2,1,0:T(8,128)(2,1)} async-done(((bf16[16,4,128,128]{3,2,1,0:T(8,128)(2,1)}), bf16[16,4,128,128]{3,2,1,0:T(8,128)(2,1)}, u32[]{:S(2)}, u32[]{:S(2)}) %all-to-all-start) | async-done | bytes 2097184 | tf_op jit(solution)/shard_map/all_to_all | solution.py:189
  112.4 5.2 %all-to-all-start.3 = ((bf16[16,4,128,128]{3,2,1,0:T(8,128)(2,1)}), bf16[16,4,128,128]{3,2,1,0:T(8,128)(2,1)}, u32[]{:S(2)}, u32[]{:S(2)}) async-start(bf16[16,4,128,128]{3,2,1,0:T(8,128)(2,1)} %attend_head.3), calls=%async_computation.3 | async-start | bytes 4194304 | tf_op jit(solution)/shard_map/all_to_all | solution.py:196
  118.5 16.5 %attend_head.2 = bf16[16,4,128,128]{3,2,1,0:T(8,128)(2,1)S(1)} custom-call(bf16[16,4,128,128]{3,2,1,0:T(8,128)(2,1)} %all-to-all-done.in_ref), custom_call_target="tpu_custom_call" | custom-call | flops 6442450944 | bytes 4194304 | tf_op jit(solution)/shard_map/attend_head/pallas_call | solution.py:71
  136.4 12.1 %collective-permute-done.8 = bf16[320,256]{1,0:T(8,128)(2,1)S(1)} collective-permute-done((bf16[320,256]{1,0:T(8,128)(2,1)S(1)}, bf16[320,256]{1,0:T(8,128)(2,1)S(1)}, u32[]{:S(2)}, u32[]{:S(2)}) %collective-permute-start.8) | collective-permute-done | bytes 163872 | tf_op jit(solution)/shard_map/ppermute | solution.py:170
  148.5 23.5 %all-to-all-done.3.in_ref = bf16[16,4,128,128]{3,2,1,0:T(8,128)(2,1)} async-done(((bf16[16,4,128,128]{3,2,1,0:T(8,128)(2,1)}), bf16[16,4,128,128]{3,2,1,0:T(8,128)(2,1)}, u32[]{:S(2)}, u32[]{:S(2)}) %all-to-all-start.3) | async-done | bytes 2097184 | tf_op jit(solution)/shard_map/all_to_all | solution.py:196
  171.9 5.2 %all-to-all-start.2 = ((bf16[16,4,128,128]{3,2,1,0:T(8,128)(2,1)}), bf16[16,4,128,128]{3,2,1,0:T(8,128)(2,1)S(1)}, u32[]{:S(2)}, u32[]{:S(2)}) async-start(bf16[16,4,128,128]{3,2,1,0:T(8,128)(2,1)} %copy-done), calls=%async_computation.2 | async-start | bytes 4194304 | tf_op jit(solution)/shard_map/all_to_all | solution.py:196
  177.9 2.8 %unpack_heads.2 = (bf16[1,128,4096]{2,1,0:T(8,128)(2,1)}, bf16[1,128,4096]{2,1,0:T(8,128)(2,1)}, bf16[1,128,4096]{2,1,0:T(8,128)(2,1)}, bf16[1,128,4096]{2,1,0:T(8,128)(2,1)}) custom-call(bf16[16,4,128,128]{3,2,1,0:T(8,128)(2,1)} %all-to-all-done.3.in_ref), custom_call_target="tpu_custom_call" | custom-call | tf_op jit(solution)/shard_map/unpack_heads/pallas_call | solution.py:126
  180.7 43.7 %all-to-all-done.2.in_ref = bf16[16,4,128,128]{3,2,1,0:T(8,128)(2,1)S(1)} async-done(((bf16[16,4,128,128]{3,2,1,0:T(8,128)(2,1)}), bf16[16,4,128,128]{3,2,1,0:T(8,128)(2,1)S(1)}, u32[]{:S(2)}, u32[]{:S(2)}) %all-to-all-start.2) | async-done | bytes 2097184 | tf_op jit(solution)/shard_map/all_to_all | solution.py:196
  224.4 1.6 unpack_heads.3
  (14 shorter events, 3.8 us)
Async XLA Ops:
  3.4 56.5 %all-to-all-start.1 = ((bf16[16,4,128,128]{3,2,1,0:T(8,128)(2,1)}), bf16[16,4,128,128]{3,2,1,0:T(8,128)(2,1)S(1)}, u32[]{:S(2)}, u32[]{:S(2)}) async-start(bf16[16,4,128,128]{3,2,1,0:T(8,128)(2,1)} %pack_heads.3), calls=%async_computation.1 | async-start | bytes 4194304 | tf_op jit(solution)/shard_map/all_to_all | solution.py:189
  14.2 9.2 %collective-permute-start.1 = (bf16[640,256]{1,0:T(8,128)(2,1)}, bf16[640,256]{1,0:T(8,128)(2,1)}, u32[]{:S(2)}, u32[]{:S(2)}) collective-permute-start(bf16[640,256]{1,0:T(8,128)(2,1)} %get-tuple-element.65), channel_id=1, source_target_pairs={{0,32},{16,48},{32,0},{48,16},{64,96},{80,112},{96,64},{112,80},{1... | collective-permute-start | bytes 983048 | tf_op jit(solution)/shard_map/ppermute | solution.py:153
  15.7 7.7 %collective-permute-start = (bf16[640,256]{1,0:T(8,128)(2,1)S(1)}, bf16[640,256]{1,0:T(8,128)(2,1)}, u32[]{:S(2)}, u32[]{:S(2)}) collective-permute-start(bf16[640,256]{1,0:T(8,128)(2,1)S(1)} %get-tuple-element.66), channel_id=1, source_target_pairs={{0,16},{16,0},{32,48},{48,32},{64,80},{80,64},{96,112},{112,96},{1... | collective-permute-start | bytes 983048 | tf_op jit(solution)/shard_map/ppermute | solution.py:153
  59.8 52.5 %all-to-all-start = ((bf16[16,4,128,128]{3,2,1,0:T(8,128)(2,1)}), bf16[16,4,128,128]{3,2,1,0:T(8,128)(2,1)}, u32[]{:S(2)}, u32[]{:S(2)}) async-start(bf16[16,4,128,128]{3,2,1,0:T(8,128)(2,1)} %pack_heads.2), calls=%async_computation | async-start | bytes 4194304 | tf_op jit(solution)/shard_map/all_to_all | solution.py:189
  64.9 25.4 %collective-permute-start.6 = (bf16[640,256]{1,0:T(8,128)(2,1)}, bf16[640,256]{1,0:T(8,128)(2,1)S(1)}, u32[]{:S(2)}, u32[]{:S(2)}) collective-permute-start(bf16[640,256]{1,0:T(8,128)(2,1)} %get-tuple-element.59), channel_id=1, source_target_pairs={{0,112},{16,96},{32,80},{48,64},{64,48},{80,32},{96,16},{112,0},{1... | collective-permute-start | bytes 983048 | tf_op jit(solution)/shard_map/ppermute | solution.py:153
  65.7 31.8 %collective-permute-start.5 = (bf16[640,256]{1,0:T(8,128)(2,1)}, bf16[640,256]{1,0:T(8,128)(2,1)S(1)}, u32[]{:S(2)}, u32[]{:S(2)}) collective-permute-start(bf16[640,256]{1,0:T(8,128)(2,1)} %get-tuple-element.60), channel_id=1, source_target_pairs={{0,96},{16,112},{32,64},{48,80},{64,32},{80,48},{96,0},{112,16},{1... | collective-permute-start | bytes 983048 | tf_op jit(solution)/shard_map/ppermute | solution.py:153
  67.8 29.6 %collective-permute-start.4 = (bf16[640,256]{1,0:T(8,128)(2,1)S(1)}, bf16[640,256]{1,0:T(8,128)(2,1)S(1)}, u32[]{:S(2)}, u32[]{:S(2)}) collective-permute-start(bf16[640,256]{1,0:T(8,128)(2,1)S(1)} %get-tuple-element.61), channel_id=1, source_target_pairs={{0,80},{16,64},{32,112},{48,96},{64,16},{80,0},{96,48},{112,32},{1... | collective-permute-start | bytes 983048 | tf_op jit(solution)/shard_map/ppermute | solution.py:153
  69.4 28.0 %collective-permute-start.3 = (bf16[640,256]{1,0:T(8,128)(2,1)S(1)}, bf16[640,256]{1,0:T(8,128)(2,1)S(1)}, u32[]{:S(2)}, u32[]{:S(2)}) collective-permute-start(bf16[640,256]{1,0:T(8,128)(2,1)S(1)} %get-tuple-element.62), channel_id=1, source_target_pairs={{0,64},{16,80},{32,96},{48,112},{64,0},{80,16},{96,32},{112,48},{1... | collective-permute-start | bytes 983048 | tf_op jit(solution)/shard_map/ppermute | solution.py:153
  71.2 26.3 %collective-permute-start.2 = (bf16[640,256]{1,0:T(8,128)(2,1)S(1)}, bf16[640,256]{1,0:T(8,128)(2,1)S(1)}, u32[]{:S(2)}, u32[]{:S(2)}) collective-permute-start(bf16[640,256]{1,0:T(8,128)(2,1)S(1)} %get-tuple-element.63), channel_id=1, source_target_pairs={{0,48},{16,32},{32,16},{48,0},{64,112},{80,96},{96,80},{112,64},{1... | collective-permute-start | bytes 983048 | tf_op jit(solution)/shard_map/ppermute | solution.py:153
  112.4 59.6 %all-to-all-start.3 = ((bf16[16,4,128,128]{3,2,1,0:T(8,128)(2,1)}), bf16[16,4,128,128]{3,2,1,0:T(8,128)(2,1)}, u32[]{:S(2)}, u32[]{:S(2)}) async-start(bf16[16,4,128,128]{3,2,1,0:T(8,128)(2,1)} %attend_head.3), calls=%async_computation.3 | async-start | bytes 4194304 | tf_op jit(solution)/shard_map/all_to_all | solution.py:196
  117.6 30.9 %collective-permute-start.8 = (bf16[320,256]{1,0:T(8,128)(2,1)S(1)}, bf16[320,256]{1,0:T(8,128)(2,1)S(1)}, u32[]{:S(2)}, u32[]{:S(2)}) collective-permute-start(bf16[320,256]{1,0:T(8,128)(2,1)S(1)} %get-tuple-element.67), channel_id=1, source_target_pairs={{0,16},{16,48},{32,80},{48,112},{64,144},{80,176},{96,208},{112,24... | collective-permute-start | bytes 491528 | tf_op jit(solution)/shard_map/ppermute | solution.py:170
  117.7 30.8 %collective-permute-start.7 = (bf16[320,256]{1,0:T(8,128)(2,1)S(1)}, bf16[320,256]{1,0:T(8,128)(2,1)S(1)}, u32[]{:S(2)}, u32[]{:S(2)}) collective-permute-start(bf16[320,256]{1,0:T(8,128)(2,1)S(1)} %get-tuple-element.68), channel_id=1, source_target_pairs={{0,0},{16,32},{32,64},{48,96},{64,128},{80,160},{96,192},{112,224}... | collective-permute-start | bytes 491528 | tf_op jit(solution)/shard_map/ppermute | solution.py:170
  135.1 1.3 copy-start
  171.9 52.5 %all-to-all-start.2 = ((bf16[16,4,128,128]{3,2,1,0:T(8,128)(2,1)}), bf16[16,4,128,128]{3,2,1,0:T(8,128)(2,1)S(1)}, u32[]{:S(2)}, u32[]{:S(2)}) async-start(bf16[16,4,128,128]{3,2,1,0:T(8,128)(2,1)} %copy-done), calls=%async_computation.2 | async-start | bytes 4194304 | tf_op jit(solution)/shard_map/all_to_all | solution.py:196
